TPU v7x, 32 devices: a whole 2x2x4 slice. The times are simulated.
32 devices in a mesh: rep: 4 (over x, core), shard: 8 (over z, y).
Axes of the slice: x: 2, y: 2, z: 4, core: 2. Of those that a mesh axis runs over, the one named last changes fastest.
Arguments:
- tokens: bfloat16 [16384, 768], P(('rep', 'shard')), may hold values from -6 to 6
- w_qkv: bfloat16 [768, 2304], P('shard'), may hold values from -0.21875 to 0.21875
- w_out: bfloat16 [768, 768], P('shard'), may hold values from -1.75 to 1.75
- w_up: bfloat16 [768, 3072], P('shard'), may hold values from -0.21875 to 0.21875
- w_down: bfloat16 [3072, 768], P('shard'), may hold values from -0.109375 to 0.109375
- gain_attn: bfloat16 [768], P('shard'), may hold values from 0.099609375 to 1.8984375
- gain_mlp: bfloat16 [768], P('shard'), may hold values from 0.099609375 to 1.8984375
- d_out: bfloat16 [16384, 768], P(('rep', 'shard')), may hold values from -6 to 6
Outputs:
- block_out: bfloat16 [16384, 768], P(('rep', 'shard'))
- d_tokens: float32 [16384, 768], P(('rep', 'shard'))
- d_w_qkv: float32 [768, 2304], P('shard')
- d_w_out: float32 [768, 768], P('shard')
- d_w_up: float32 [768, 3072], P('shard')
- d_w_down: float32 [3072, 768], P('shard')
- d_gain_attn: float32 [768], P('shard')
- d_gain_mlp: float32 [768], P('shard')
All inputs are finite; a program needn't handle non-finite values.
Results may differ from a plain program's by a relative error of at most 0.015.
Values may be sent and summed in bfloat16 or wider, within the bound.
No kernel may reach another device: no remote copies, remote signals or barrier semaphores. Data moves between devices by JAX's collectives and lax.ppermute only.
A program may use at most 256 MiB of HBM per device.

v0:
```python
import jax
import jax.numpy as jnp
from jax import lax
from jax.sharding import PartitionSpec as P

D = 768
HEADS = 12
HDIM = 64
GROUPS_DEV = 2
PLEN = 1024
CLEN = 128
CONTS = 8
PR_DEV = 128


norm_eps = 1e-05
neg_fill = -1e30


def partner_2(shard, axis, stride):
    return lax.ppermute(shard, axis, [(i, i ^ 1 << stride) for i in range(lax.axis_size(axis))])


def rms_scale(values, gain_vec):
    return (
        values * lax.rsqrt(jnp.mean(values * values, axis=-1, keepdims=True) + norm_eps) * gain_vec
    )


def gelu_tanh(values):
    return jax.nn.gelu(values, approximate=True)


def to_groups(values):
    col_width = values.shape[1]
    prompt_rows = GROUPS_DEV * PR_DEV
    head_rows = values[:prompt_rows].reshape(GROUPS_DEV, PR_DEV, col_width)
    tail_rows = values[prompt_rows:].reshape(GROUPS_DEV, CLEN, col_width)
    return jnp.concatenate([head_rows, tail_rows], axis=1)


def to_tokens(values):
    col_width = values.shape[-1]
    head_rows = values[:, :PR_DEV].reshape(GROUPS_DEV * PR_DEV, col_width)
    tail_rows = values[:, PR_DEV:].reshape(GROUPS_DEV * CLEN, col_width)
    return jnp.concatenate([head_rows, tail_rows], axis=0)


def split_heads(values):
    return values.reshape(values.shape[0], values.shape[1], HEADS, HDIM)


def visible_mask(offset):
    row_ids = lax.broadcasted_iota(jnp.int32, (PR_DEV + CLEN, PLEN + CLEN), 0)
    col_ids = lax.broadcasted_iota(jnp.int32, (PR_DEV + CLEN, PLEN + CLEN), 1)
    prompt_seen = (col_ids < PLEN) & (col_ids <= offset * PR_DEV + row_ids)
    cont_seen = (col_ids < PLEN) | (col_ids - PLEN <= row_ids - PR_DEV)
    return jnp.where(row_ids < PR_DEV, prompt_seen, cont_seen)


def block_scores(queries, kv_pairs, visible):
    query_heads = split_heads(queries)
    key_heads = split_heads(kv_pairs[..., :D])
    scores = jnp.einsum(
        "brhd,bkhd->bhrk", query_heads, key_heads, preferred_element_type=jnp.float32
    ) * HDIM ** (-0.5)
    return jnp.where(visible, scores, neg_fill)


def attend(queries, kv_pairs, visible):
    scores = block_scores(queries, kv_pairs, visible)
    row_max = jnp.max(scores, axis=-1, keepdims=True)
    exp_terms = jnp.exp(scores - row_max)
    row_total = jnp.sum(exp_terms, axis=-1, keepdims=True)
    soft_weights = (exp_terms / row_total).astype(jnp.bfloat16)
    value_heads = split_heads(kv_pairs[..., D:])
    attended = jnp.einsum(
        "bhrk,bkhd->brhd", soft_weights, value_heads, preferred_element_type=jnp.float32
    )
    return (attended.reshape(queries.shape), row_max + jnp.log(row_total))


def attend_back(queries, kv_pairs, visible, log_total, d_block):
    scores = block_scores(queries, kv_pairs, visible)
    soft_full = jnp.exp(scores - log_total)
    query_heads = split_heads(queries)
    key_heads = split_heads(kv_pairs[..., :D])
    value_heads = split_heads(kv_pairs[..., D:])
    grad_heads = split_heads(d_block)
    d_soft = jnp.einsum(
        "brhd,bkhd->bhrk", grad_heads, value_heads, preferred_element_type=jnp.float32
    )
    delta_rows = jnp.sum(soft_full * d_soft, axis=-1, keepdims=True)
    d_scores = (soft_full * (d_soft - delta_rows)).astype(jnp.bfloat16)
    score_scale = HDIM ** (-0.5)
    d_query = (
        jnp.einsum("bhrk,bkhd->brhd", d_scores, key_heads, preferred_element_type=jnp.float32)
        * score_scale
    )
    d_key = (
        jnp.einsum("bhrk,brhd->bkhd", d_scores, query_heads, preferred_element_type=jnp.float32)
        * score_scale
    )
    d_value = jnp.einsum(
        "bhrk,brhd->bkhd",
        soft_full.astype(jnp.bfloat16),
        grad_heads,
        preferred_element_type=jnp.float32,
    )
    key_shape = (kv_pairs.shape[0], kv_pairs.shape[1], D)
    d_pair = jnp.concatenate([d_key.reshape(key_shape), d_value.reshape(key_shape)], axis=-1)
    return (d_query.reshape(queries.shape), d_pair)


def per_device(tokens, w_qkv, w_out, w_up, w_down, gain_attn, gain_mlp, d_out):
    full_qkv, full_out, full_up, full_down, full_gain_attn, full_gain_mlp = (
        lax.all_gather(w_qkv, "shard", axis=0, tiled=True),
        lax.all_gather(w_out, "shard", axis=0, tiled=True),
        lax.all_gather(w_up, "shard", axis=0, tiled=True),
        lax.all_gather(w_down, "shard", axis=0, tiled=True),
        lax.all_gather(gain_attn, "shard", axis=0, tiled=True),
        lax.all_gather(gain_mlp, "shard", axis=0, tiled=True),
    )
    token_rows = tokens.astype(jnp.float32)
    attn_gain = full_gain_attn.astype(jnp.float32)
    mlp_gain = full_gain_mlp.astype(jnp.float32)
    normed = rms_scale(token_rows, attn_gain).astype(jnp.bfloat16)
    qkv_rows = jnp.dot(normed, full_qkv, preferred_element_type=jnp.float32).astype(jnp.bfloat16)
    group_queries = to_groups(qkv_rows[:, :D])
    own_pairs = to_groups(qkv_rows[:, D:])
    offset = lax.axis_index("shard") % CONTS
    levels = CONTS.bit_length() - 1
    shared = own_pairs[:, :PR_DEV][None]
    for level_bit in range(levels):
        partner = partner_2(shared, "shard", level_bit)
        is_upper = jnp.right_shift(offset, level_bit) % 2 == 1
        shared = jnp.where(
            is_upper,
            jnp.concatenate([partner, shared], axis=0),
            jnp.concatenate([shared, partner], axis=0),
        )
    prompt_pairs = shared.transpose(1, 0, 2, 3).reshape(GROUPS_DEV, PLEN, 2 * D)
    kv_pairs = jnp.concatenate([prompt_pairs, own_pairs[:, PR_DEV:]], axis=1)
    visible = visible_mask(offset)
    block_size = min(GROUPS_DEV, 2)
    attended, log_total = attend(group_queries, kv_pairs, visible)
    log_totals = [log_total]
    attn_rows = to_tokens(attended).astype(jnp.bfloat16)
    middle = token_rows + jnp.dot(attn_rows, full_out, preferred_element_type=jnp.float32)
    normed_mlp = rms_scale(middle, mlp_gain).astype(jnp.bfloat16)
    hidden = jnp.dot(normed_mlp, full_up, preferred_element_type=jnp.float32)
    active = gelu_tanh(hidden).astype(jnp.bfloat16)
    block_out = (middle + jnp.dot(active, full_down, preferred_element_type=jnp.float32)).astype(
        jnp.bfloat16
    )
    full_qkv, full_out, full_up, full_down = (
        lax.all_gather(w_qkv, "shard", axis=0, tiled=True),
        lax.all_gather(w_out, "shard", axis=0, tiled=True),
        lax.all_gather(w_up, "shard", axis=0, tiled=True),
        lax.all_gather(w_down, "shard", axis=0, tiled=True),
    )
    d_down = jnp.einsum("tf,td->fd", active, d_out, preferred_element_type=jnp.float32)
    d_active = jnp.einsum("td,fd->tf", d_out, full_down, preferred_element_type=jnp.float32)
    _, gelu_pull = jax.vjp(gelu_tanh, hidden)
    d_hidden = gelu_pull(d_active)[0].astype(jnp.bfloat16)
    d_up = jnp.einsum("tc,tf->cf", normed_mlp, d_hidden, preferred_element_type=jnp.float32)
    d_normed_mlp = jnp.einsum("tf,cf->tc", d_hidden, full_up, preferred_element_type=jnp.float32)
    _, mlp_norm_pull = jax.vjp(rms_scale, middle, mlp_gain)
    d_middle_part, d_gain_mlp = mlp_norm_pull(d_normed_mlp)
    d_middle = d_out.astype(jnp.float32) + d_middle_part
    d_branch = d_middle.astype(jnp.bfloat16)
    d_attn_out = jnp.einsum("tc,td->cd", attn_rows, d_branch, preferred_element_type=jnp.float32)
    d_attended = jnp.einsum(
        "td,cd->tc", d_branch, full_out, preferred_element_type=jnp.float32
    ).astype(jnp.bfloat16)
    group_grads = to_groups(d_attended)
    d_query, d_pair = attend_back(
        group_queries, kv_pairs, visible, log_totals[0 // block_size], group_grads
    )
    pending = d_pair[:, :PLEN].reshape(GROUPS_DEV, CONTS, PR_DEV, 2 * D).transpose(1, 0, 2, 3)
    for level_bit in reversed(range(levels)):
        half_size = pending.shape[0] // 2
        is_upper = jnp.right_shift(offset, level_bit) % 2 == 1
        kept_half = jnp.where(is_upper, pending[half_size:], pending[:half_size])
        sent_half = jnp.where(is_upper, pending[:half_size], pending[half_size:])
        pending = kept_half + partner_2(sent_half.astype(jnp.bfloat16), "shard", level_bit).astype(
            sent_half.dtype
        )
    d_own_pairs = jnp.concatenate([pending[0], d_pair[:, PLEN:]], axis=1)
    d_qkv = jnp.concatenate([to_tokens(d_query), to_tokens(d_own_pairs)], axis=1).astype(
        jnp.bfloat16
    )
    d_qkv_w = jnp.einsum("tc,tq->cq", normed, d_qkv, preferred_element_type=jnp.float32)
    d_normed = jnp.einsum("tq,cq->tc", d_qkv, full_qkv, preferred_element_type=jnp.float32)
    _, attn_norm_pull = jax.vjp(rms_scale, token_rows, attn_gain)
    d_token_part, d_gain_attn = attn_norm_pull(d_normed)
    d_tokens = d_middle + d_token_part
    summed = (
        lax.psum_scatter(d_qkv_w, "shard", scatter_dimension=0, tiled=True),
        lax.psum_scatter(d_attn_out, "shard", scatter_dimension=0, tiled=True),
        lax.psum_scatter(d_up, "shard", scatter_dimension=0, tiled=True),
        lax.psum_scatter(d_down, "shard", scatter_dimension=0, tiled=True),
        lax.psum_scatter(d_gain_attn, "shard", scatter_dimension=0, tiled=True),
        lax.psum_scatter(d_gain_mlp, "shard", scatter_dimension=0, tiled=True),
    )
    replica_sums = (
        lax.psum(summed[0].astype(jnp.bfloat16), "rep").astype(jnp.float32),
        lax.psum(summed[1].astype(jnp.bfloat16), "rep").astype(jnp.float32),
        lax.psum(summed[2].astype(jnp.bfloat16), "rep").astype(jnp.float32),
        lax.psum(summed[3].astype(jnp.bfloat16), "rep").astype(jnp.float32),
        lax.psum(summed[4].astype(jnp.bfloat16), "rep").astype(jnp.float32),
        lax.psum(summed[5].astype(jnp.bfloat16), "rep").astype(jnp.float32),
    )
    return (
        block_out,
        d_tokens,
        replica_sums[0],
        replica_sums[1],
        replica_sums[2],
        replica_sums[3],
        replica_sums[4],
        replica_sums[5],
    )


def solution(mesh):
    return jax.shard_map(
        per_device,
        mesh=mesh,
        in_specs=(
            P(("rep", "shard"), None),
            P("shard", None),
            P("shard", None),
            P("shard", None),
            P("shard", None),
            P("shard"),
            P("shard"),
            P(("rep", "shard"), None),
        ),
        out_specs=(
            P(("rep", "shard"), None),
            P(("rep", "shard"), None),
            P("shard", None),
            P("shard", None),
            P("shard", None),
            P("shard", None),
            P("shard"),
            P("shard"),
        ),
        check_vma=False,
    )
```

profile of v0, /device:TPU:0, one launch (start us, length us, event | category | flops | bytes accessed | tf_op | source)
XLA Modules:
  0.0 1178.0 jit_solution(297730338307355292)
XLA Ops:
  12.4 23.3 %all-reduce.5 = (bf16[768]{0:T(1024)(128)(2,1)S(1)}, bf16[768]{0:T(1024)(128)(2,1)S(1)}) all-reduce(bf16[768]{0:T(1024)(128)(2,1)S(1)} %dynamic-update-slice, bf16[768]{0:T(1024)(128)(2,1)S(1)} %dynamic-update-slice.1), channel_id=1, replica_groups=mesh['rep'=4,'shard'=8] {'shard'}, use_global_device_ids=true, to_apply=%add | all-reduce | flops 1536 | bytes 6144
  37.6 40.7 %all-gather.5.cloned.1.call-done = bf16[768,2304]{1,0:T(8,128)(2,1)} async-done(((bf16[96,2304]{1,0:T(8,128)(2,1)}), bf16[768,2304]{1,0:T(8,128)(2,1)}) %all-gather.5.cloned.1.call-update) | async-done | bytes 3538960 | tf_op jit(solution)/shard_map/all_gather | solution.py:117
  84.9 24.1 %collective-permute-done = bf16[1,2,128,1536]{3,2,0,1:T(8,128)(2,1)S(1)} collective-permute-done((bf16[1,2,128,1536]{3,2,0,1:T(8,128)(2,1)S(1)}, bf16[1,2,128,1536]{3,2,0,1:T(8,128)(2,1)S(1)}, u32[]{:S(2)}, u32[]{:S(2)}) %collective-permute-start) | collective-permute-done | bytes 786464 | tf_op jit(solution)/shard_map/ppermute | solution.py:21
  110.4 74.7 %collective-permute-done.1 = bf16[2,2,128,1536]{3,2,0,1:T(8,128)(2,1)} collective-permute-done((bf16[2,2,128,1536]{3,2,0,1:T(8,128)(2,1)S(1)}, bf16[2,2,128,1536]{3,2,0,1:T(8,128)(2,1)}, u32[]{:S(2)}, u32[]{:S(2)}) %collective-permute-start.1) | collective-permute-done | bytes 1572896 | tf_op jit(solution)/shard_map/ppermute | solution.py:21
  208.4 122.8 %collective-permute-done.2 = bf16[4,2,128,1536]{3,2,0,1:T(8,128)(2,1)} collective-permute-done((bf16[4,2,128,1536]{3,2,0,1:T(8,128)(2,1)S(1)}, bf16[4,2,128,1536]{3,2,0,1:T(8,128)(2,1)}, u32[]{:S(2)}, u32[]{:S(2)}) %collective-permute-start.2) | collective-permute-done | bytes 3145760 | tf_op jit(solution)/shard_map/ppermute | solution.py:21
  349.3 12.7 %fusion.49 = (f32[2,12,256]{2,1,0:T(8,128)S(1)}, f32[2,12,256,1152]{3,2,1,0:T(8,128)}) fusion(bf16[2,256,12,64]{1,3,2,0:T(8,128)(2,1)} %copy_dynamic-update-slice_fusion.2, bf16[2,1152,12,64]{1,3,2,0:T(8,128)(2,1)S(1)} %bitcast.66, pred[256,1152]{1,0:T(8,128)(4,1)} %fusion.26), kind=kOutput, calls=%fused_computation.105 | convolution fusion | flops 927197184 | bytes 32956416 | tf_op jit(solution)/shard_map/brhd,bkhd->bhrk/dot_general | solution.py:64
  361.9 10.9 fusion
  372.8 12.3 %fusion.24 = bf16[2,12,64,256]{3,2,1,0:T(8,128)(2,1)} fusion(bf16[2,1152,12,64]{1,3,2,0:T(8,128)(2,1)S(1)} %bitcast.71, f32[2,12,256,1152]{3,2,1,0:T(8,128)} %get-tuple-element.37, f32[2,12,256]{2,1,0:T(8,128)} %fusion, f32[2,12,256]{2,1,0:T(8,128)} %copy-done.24), kind=kOutput, calls=%fused_computation.64 | convolution fusion | flops 927596544 | bytes 32686080 | tf_op jit(solution)/shard_map/bhrk,bkhd->brhd/dot_general | solution.py:77
  389.4 41.4 %all-gather.9.cloned.1.call-done = bf16[768,3072]{1,0:T(8,128)(2,1)} async-done(((bf16[96,3072]{1,0:T(8,128)(2,1)}), bf16[768,3072]{1,0:T(8,128)(2,1)}) %all-gather.9.cloned.1.call-update) | async-done | bytes 4718608 | tf_op jit(solution)/shard_map/all_gather | solution.py:119
  430.8 12.5 %fusion.13 = (bf16[512,3072]{1,0:T(8,128)(2,1)S(1)}, f32[512,3072]{1,0:T(8,128)}) fusion(f32[512,3072]{1,0:T(8,128)} %fusion.50, bf16[768,3072]{1,0:T(8,128)(2,1)} %all-gather.9.cloned.1.call-done, f32[512,768]{1,0:T(8,128)S(1)} %get-tuple-element.39, f32[768]{0:T(1024)S(1)} %convert_element_type.106, f32[512]{0:T(512)S(1)} %fusion.35), kind=kOutput, calls=%fused_computation.24 | convolution fusion | flops 2448556032 | bytes 22025216 | tf_op jit(solution)/shard_map/dot_general | solution.py:151
  449.4 9.9 fusion.42
  470.0 15.1 %fusion.2 = f32[2,12,64,1152]{3,2,1,0:T(8,128)} fusion(bf16[2,256,12,64]{1,3,2,0:T(8,128)(2,1)S(1)} %copy_dynamic-update-slice_fusion, f32[2,12,256,1152]{3,2,1,0:T(8,128)} %get-tuple-element.37, f32[2,12,256]{2,1,0:T(8,128)S(1)} %log_add_fusion), kind=kOutput, calls=%fused_computation.8 | convolution fusion | flops 920125440 | bytes 36200448 | tf_op jit(solution)/shard_map/bhrk,brhd->bkhd/dot_general | solution.py:104
  493.4 26.4 %multiply_reduce_fusion = (f32[2,12,256]{2,1,0:T(8,128)S(1)}, f32[2,12,256,1152]{3,2,1,0:T(8,128)}) fusion(f32[2,12,256,1152]{3,2,1,0:T(8,128)} %get-tuple-element.37, f32[2,12,256]{2,1,0:T(8,128)} %copy-done.21, bf16[2,256,12,64]{1,3,2,0:T(8,128)(2,1)} %copy-done.11, bf16[2,1152,12,64]{1,3,2,0:T(8,128)(2,1)S(1)} %bitcast.72), kind=kOutput, calls=%fused_computation.1 | convolution fusion | flops 927197184 | bytes 60997632 | tf_op jit(solution)/shard_map/brhd,bkhd->bhrk/dot_general | solution.py:90
  519.8 24.1 %multiply_convert_fusion = bf16[2,12,256,1152]{3,2,1,0:T(8,128)(2,1)} fusion(f32[2,12,256,1152]{3,2,1,0:T(8,128)} %get-tuple-element.44, f32[2,12,256,1152]{3,2,1,0:T(8,128)} %get-tuple-element.37, f32[2,12,256]{2,1,0:T(8,128)S(1)} %get-tuple-element.43, f32[2,12,256]{2,1,0:T(8,128)S(1)} %copy-done.22), kind=kLoop, calls=%fused_computation | loop fusion | flops 28311552 | bytes 70828032 | tf_op jit(solution)/shard_map/convert_element_type | solution.py:94
  543.9 10.6 convolution_multiply_fusion
  570.9 203.0 %collective-permute-done.3 = bf16[4,2,128,1536]{3,2,0,1:T(8,128)(2,1)} collective-permute-done((bf16[4,2,128,1536]{3,2,0,1:T(8,128)(2,1)S(1)}, bf16[4,2,128,1536]{3,2,0,1:T(8,128)(2,1)}, u32[]{:S(2)}, u32[]{:S(2)}) %collective-permute-start.3) | collective-permute-done | bytes 3145760 | tf_op jit(solution)/shard_map/ppermute | solution.py:21
  783.5 99.2 %collective-permute-done.4 = bf16[2,2,128,1536]{3,2,0,1:T(8,128)(2,1)S(1)} collective-permute-done((bf16[2,2,128,1536]{3,2,0,1:T(8,128)(2,1)S(1)}, bf16[2,2,128,1536]{3,2,0,1:T(8,128)(2,1)S(1)}, u32[]{:S(2)}, u32[]{:S(2)}) %collective-permute-start.4) | collective-permute-done | bytes 1572896 | tf_op jit(solution)/shard_map/ppermute | solution.py:21
  890.5 10.6 multiply_convert_fusion.2
  904.4 11.9 %collective-permute-done.5 = bf16[1,2,128,1536]{3,2,0,1:T(8,128)(2,1)} collective-permute-done((bf16[1,2,128,1536]{3,2,0,1:T(8,128)(2,1)}, bf16[1,2,128,1536]{3,2,0,1:T(8,128)(2,1)}, u32[]{:S(2)}, u32[]{:S(2)}) %collective-permute-start.5) | collective-permute-done | bytes 786464 | tf_op jit(solution)/shard_map/ppermute | solution.py:21
  925.2 8.8 add_convert_fusion.1
  937.7 45.6 %reduce-scatter.9.cloned.1.call-done = f32[96,3072]{1,0:T(8,128)} async-done(((f32[768,3072]{1,0:T(8,128)}), f32[96,3072]{1,0:T(8,128)}) %reduce-scatter.9.cloned.1.call-update) | async-done | bytes 1179664 | tf_op jit(solution)/shard_map/reduce_scatter | solution.py:201
  985.5 129.7 %reduce-scatter.5.cloned.1.call-done = f32[96,2304]{1,0:T(8,128)} async-done(((f32[768,2304]{1,0:T(8,128)}), f32[96,2304]{1,0:T(8,128)}) %reduce-scatter.5.cloned.1.call-update) | async-done | bytes 884752 | tf_op jit(solution)/shard_map/reduce_scatter | solution.py:199
  1123.6 19.8 %all-reduce.4 = (bf16[768]{0:T(1024)(128)(2,1)S(1)}, bf16[768]{0:T(1024)(128)(2,1)S(1)}) all-reduce(f32[768]{0:T(1024)} %get-tuple-element.10, f32[768]{0:T(1024)S(1)} %get-tuple-element.8), channel_id=6, replica_groups=mesh['rep'=4,'shard'=8] {'shard'}, use_global_device_ids=true, to_apply=%region_16.17.clone | all-reduce | flops 1536 | bytes 9216
  1153.9 10.4 all-reduce.10.cloned.1.call-done
  (175 shorter events, 161.6 us)
Async XLA Ops:
  7.2 71.1 %all-gather.5.cloned.1.call-start = ((), (), s32[]{:S(2)}) async-start(), calls=%async_computation.4 | async-start | bytes 3981312 | tf_op jit(solution)/shard_map/all_gather | solution.py:117
  7.9 192.6 %all-gather.11.cloned.1.call-start = ((), (), s32[]{:S(2)}) async-start(), calls=%async_computation.7 | async-start | bytes 5308416 | tf_op jit(solution)/shard_map/all_gather | solution.py:120
  8.6 378.1 %all-gather.7.cloned.1.call-start = ((), (), s32[]{:S(2)}) async-start(), calls=%async_computation.5 | async-start | bytes 1327104 | tf_op jit(solution)/shard_map/all_gather | solution.py:118
  35.6 47.0 %copy-start.29 = (f32[768]{0:T(1024)}, f32[768]{0:T(1024)S(1)}, u32[]{:S(2)}) copy-start(f32[768]{0:T(1024)S(1)} %convert_element_type.102) | copy-start | bytes 9220
  37.6 45.0 %copy-start.31 = (f32[512]{0:T(512)}, f32[512]{0:T(512)S(1)}, u32[]{:S(2)}) copy-start(f32[512]{0:T(512)S(1)} %fusion.34) | copy-start | bytes 6148
  84.4 24.6 %collective-permute-start = (bf16[1,2,128,1536]{3,2,0,1:T(8,128)(2,1)S(1)}, bf16[1,2,128,1536]{3,2,0,1:T(8,128)(2,1)S(1)}, u32[]{:S(2)}, u32[]{:S(2)}) collective-permute-start(bf16[1,2,128,1536]{3,2,0,1:T(8,128)(2,1)S(1)} %bitcast.75), channel_id=1, source_target_pairs={{0,1},{1,0},{2,3},{3,2},{4,5},{5,4},{6,7},{7,6},{8,9},{9,8},{10,11... | collective-permute-start | bytes 2359304 | tf_op jit(solution)/shard_map/ppermute | solution.py:21
  109.3 75.8 %collective-permute-start.1 = (bf16[2,2,128,1536]{3,2,0,1:T(8,128)(2,1)S(1)}, bf16[2,2,128,1536]{3,2,0,1:T(8,128)(2,1)}, u32[]{:S(2)}, u32[]{:S(2)}) collective-permute-start(bf16[2,2,128,1536]{3,2,0,1:T(8,128)(2,1)S(1)} %maximum_select_fusion.2), channel_id=1, source_target_pairs={{0,2},{1,3},{2,0},{3,1},{4,6},{5,7},{6,4},{7,5},{8,10},{9,11},{10,... | collective-permute-start | bytes 4718600 | tf_op jit(solution)/shard_map/ppermute | solution.py:21
  110.3 320.5 %all-gather.9.cloned.1.call-start = ((), (), s32[]{:S(2)}) async-start(), calls=%async_computation.6 | async-start | bytes 5308416 | tf_op jit(solution)/shard_map/all_gather | solution.py:119
  188.4 142.8 %collective-permute-start.2 = (bf16[4,2,128,1536]{3,2,0,1:T(8,128)(2,1)S(1)}, bf16[4,2,128,1536]{3,2,0,1:T(8,128)(2,1)}, u32[]{:S(2)}, u32[]{:S(2)}) collective-permute-start(bf16[4,2,128,1536]{3,2,0,1:T(8,128)(2,1)S(1)} %maximum_select_fusion.1), channel_id=1, source_target_pairs={{0,4},{1,5},{2,6},{3,7},{4,0},{5,1},{6,2},{7,3},{8,12},{9,13},{10,... | collective-permute-start | bytes 9437192 | tf_op jit(solution)/shard_map/ppermute | solution.py:21
  188.8 745.1 %reduce-scatter.7.cloned.1.call-start = ((), (), s32[]{:S(2)}) async-start(), calls=%async_computation.9 | async-start | bytes 2654208 | tf_op jit(solution)/shard_map/reduce_scatter | solution.py:200
  208.4 127.1 %copy-start.12 = (bf16[256,1536]{1,0:T(8,128)(2,1)S(1)}, bf16[256,1536]{1,0:T(8,128)(2,1)}, u32[]{:S(2)}) copy-start(bf16[256,1536]{1,0:T(8,128)(2,1)} %get-tuple-element.26) | copy-start | bytes 2359300
  386.7 56.5 %copy-start.16 = (bf16[2,128,768]{2,1,0:T(8,128)(2,1)}, bf16[2,128,768]{2,1,0:T(8,128)(2,1)S(1)}, u32[]{:S(2)}) copy-start(bf16[2,128,768]{2,1,0:T(8,128)(2,1)S(1)} %copy.79) | copy-start | bytes 1179652
  389.4 73.0 %copy-start.8 = (f32[512,768]{1,0:T(8,128)}, f32[512,768]{1,0:T(8,128)S(1)}, u32[]{:S(2)}) copy-start(f32[512,768]{1,0:T(8,128)S(1)} %get-tuple-element.39) | copy-start | bytes 4718596
  449.4 486.2 %reduce-scatter.11.cloned.1.call-start = ((), (), s32[]{:S(2)}) async-start(), calls=%async_computation.11 | async-start | bytes 10616832 | tf_op jit(solution)/shard_map/reduce_scatter | solution.py:202
  459.3 524.0 %reduce-scatter.9.cloned.1.call-start = ((), (), s32[]{:S(2)}) async-start(), calls=%async_computation.10 | async-start | bytes 10616832 | tf_op jit(solution)/shard_map/reduce_scatter | solution.py:201
  469.9 645.3 %reduce-scatter.5.cloned.1.call-start = ((), (), s32[]{:S(2)}) async-start(), calls=%async_computation.8 | async-start | bytes 7962624 | tf_op jit(solution)/shard_map/reduce_scatter | solution.py:199
  493.4 26.4 %copy-start.22 = (f32[2,12,256]{2,1,0:T(8,128)S(1)}, f32[2,12,256]{2,1,0:T(8,128)}, u32[]{:S(2)}) copy-start(f32[2,12,256]{2,1,0:T(8,128)} %copy-done.21) | copy-start | bytes 73732
  569.3 204.7 %collective-permute-start.3 = (bf16[4,2,128,1536]{3,2,0,1:T(8,128)(2,1)S(1)}, bf16[4,2,128,1536]{3,2,0,1:T(8,128)(2,1)}, u32[]{:S(2)}, u32[]{:S(2)}) collective-permute-start(bf16[4,2,128,1536]{3,2,0,1:T(8,128)(2,1)S(1)} %select_convert_fusion), channel_id=1, source_target_pairs={{0,4},{1,5},{2,6},{3,7},{4,0},{5,1},{6,2},{7,3},{8,12},{9,13},{10,... | collective-permute-start | bytes 9437192 | tf_op jit(solution)/shard_map/ppermute | solution.py:21
  783.4 99.3 %collective-permute-start.4 = (bf16[2,2,128,1536]{3,2,0,1:T(8,128)(2,1)S(1)}, bf16[2,2,128,1536]{3,2,0,1:T(8,128)(2,1)S(1)}, u32[]{:S(2)}, u32[]{:S(2)}) collective-permute-start(bf16[2,2,128,1536]{3,2,0,1:T(8,128)(2,1)S(1)} %select_convert_fusion.1), channel_id=1, source_target_pairs={{0,2},{1,3},{2,0},{3,1},{4,6},{5,7},{6,4},{7,5},{8,10},{9,11},{10,... | collective-permute-start | bytes 4718600 | tf_op jit(solution)/shard_map/ppermute | solution.py:21
  889.4 26.9 %collective-permute-start.5 = (bf16[1,2,128,1536]{3,2,0,1:T(8,128)(2,1)}, bf16[1,2,128,1536]{3,2,0,1:T(8,128)(2,1)}, u32[]{:S(2)}, u32[]{:S(2)}) collective-permute-start(bf16[1,2,128,1536]{3,2,0,1:T(8,128)(2,1)} %select_convert_fusion.2), channel_id=1, source_target_pairs={{0,1},{1,0},{2,3},{3,2},{4,5},{5,4},{6,7},{7,6},{8,9},{9,8},{10,11... | collective-permute-start | bytes 2359304 | tf_op jit(solution)/shard_map/ppermute | solution.py:21
  902.7 15.2 %copy-start.23 = (bf16[2,128,768]{2,1,0:T(8,128)(2,1)}, bf16[2,128,768]{2,1,0:T(8,128)(2,1)S(1)}, u32[]{:S(2)}) copy-start(bf16[2,128,768]{2,1,0:T(8,128)(2,1)S(1)} %copy.81) | copy-start | bytes 1179652
  923.8 240.5 %all-reduce.10.cloned.1.call-start = ((), (), s32[]{:S(2)}) async-start(), calls=%async_computation.12 | async-start | bytes 3538944 | tf_op jit(solution)/shard_map/psum | solution.py:207
  1117.2 33.0 %copy-start.28 = (f32[512]{0:T(512)S(1)}, f32[512]{0:T(512)}, u32[]{:S(2)}) copy-start(f32[512]{0:T(512)} %copy-done.27) | copy-start | bytes 6148
  1117.2 33.7 %copy-start.5 = (f32[512,768]{1,0:T(8,128)S(1)}, f32[512,768]{1,0:T(8,128)}, u32[]{:S(2)}) copy-start(f32[512,768]{1,0:T(8,128)} %copy-done.4) | copy-start | bytes 4718596
  (25 other events, 166.7 us)
Sparse Core Ops, SparseCore 0:
  10.2 68.0 all-gather.4
  80.5 102.6 all-gather.10
  185.4 164.6 all-gather.6
  352.1 78.6 all-gather.8
  449.5 67.0 reduce-scatter.6
  520.1 260.2 reduce-scatter.10
  783.9 199.3 reduce-scatter.8
  987.0 128.1 reduce-scatter.4
  1118.6 45.6 all-reduce.9
where the time goes:
time: 1180 us
  waiting for transfers between devices  805 us (68%)
  matrix products  160 us (14%)
  other arithmetic  93 us (8%)
  local copies, waits for them, and re-layouts  50.3 us (4%)
  blocking collectives  48.7 us (4%)
  between operations  16.2 us (1%)
    ppermute x6, waiting for transfers between devices, partner_2(): lax.ppermute(shard, axis, [(i, i ^ 1 << stride) for i in range(lax.axis_s...  536 us
    reduce_scatter x1, waiting for transfers between devices, per_device(): lax.psum_scatter(d_qkv_w, 'shard', scatter_dimension=0, tiled=True)  130 us
    reduce_scatter x1, waiting for transfers between devices, per_device(): lax.psum_scatter(d_up, 'shard', scatter_dimension=0, tiled=True)  45.6 us
    unnamed x2, blocking collectives  43.1 us
    all_gather x1, waiting for transfers between devices, per_device(): lax.all_gather(w_up, 'shard', axis=0, tiled=True)  41.4 us
    all_gather x1, waiting for transfers between devices, per_device(): lax.all_gather(w_qkv, 'shard', axis=0, tiled=True)  40.7 us
    dot_general x1, matrix products, attend_back(): jnp.einsum('brhd,bkhd->bhrk', grad_heads, value_heads, preferred_element_...  26.4 us
    convert_element_type x1, other arithmetic, attend_back(): d_scores = (soft_full * (d_soft - delta_rows)).astype(jnp.bfloat16)  24.1 us
  transfers between devices with their start and end apart: 15, of which 11 were waited for; matrix products, arithmetic and copies ran while one was open for 23% of the time, Pallas kernels for 0%

commit v1 on v0

v1 whole, which is shorter than its diff:
```python
import functools

import jax
import jax.numpy as jnp
from jax import lax
from jax.experimental import pallas as pl
from jax.experimental.pallas import tpu as pltpu
from jax.sharding import PartitionSpec as P

D = 768
HEADS = 12
HDIM = 64
FF = 3072
PR = 128
PLEN = 1024
KEYS = PLEN + 2 * PR
ROWS = 4 * PR
PAIRS = HEADS // 2
FCHUNK = 512
norm_eps = 1e-05
neg_fill = -1e30
SCALE = HDIM ** (-0.5)
GELU_C = 0.7978845608028654
GELU_A = 0.044715
BF = jnp.bfloat16
F32 = jnp.float32
VMEM_LIMIT = 60 * 1024 * 1024


def dot_nt(a, b):
    return lax.dot_general(a, b, (((1,), (1,)), ((), ())), preferred_element_type=F32)


def dot_tn(a, b):
    return lax.dot_general(a, b, (((0,), (0,)), ((), ())), preferred_element_type=F32)


def dot_nn(a, b):
    return jnp.dot(a, b, preferred_element_type=F32)


def rms_inv(values):
    return lax.rsqrt(jnp.mean(values * values, axis=-1, keepdims=True) + norm_eps)


def fill_normed(x_ref, gain_ref, normed_ref):
    gain = gain_ref[...]

    @pl.loop(0, KEYS, step=PR)
    def _(row):
        rows = pl.ds(pl.multiple_of(row, PR), PR)
        part = x_ref[rows, :].astype(F32)
        normed_ref[rows, :] = (part * rms_inv(part) * gain).astype(BF)


def lane_half(head):
    lanes = lax.broadcasted_iota(jnp.int32, (1, 2 * HDIM), 1)
    return (lanes >= HDIM) if head else (lanes < HDIM)


def attn_fwd_kernel(
    pos_ref, x_ref, gain_ref, wq_ref, wk_ref, wv_ref,
    q_ref, k_ref, v_ref, e_ref, ec_ref, o_ref, r_ref,
    normed_ref, bias_ref,
):
    @pl.when(pl.program_id(0) == 0)
    def _():
        fill_normed(x_ref, gain_ref, normed_ref)
        pos = pos_ref[0]
        row = lax.broadcasted_iota(jnp.int32, (PR, PR), 0)
        col = lax.broadcasted_iota(jnp.int32, (PR, PR), 1)
        tri = jnp.where(col <= row, 0.0, neg_fill)
        for part in range(2):
            mine = jnp.bitwise_xor(pos, part)
            for block in range(8):
                at = (pl.ds(part * PR, PR), pl.ds(block * PR, PR))
                if block == part:
                    bias_ref[at] = tri
                else:
                    seen = jnp.bitwise_xor(pos, block) < mine
                    bias_ref[at] = jnp.full((PR, PR), jnp.where(seen, 0.0, neg_fill), F32)

    keys = dot_nn(normed_ref[...], wk_ref[...]).astype(BF)
    values = dot_nn(normed_ref[...], wv_ref[...]).astype(BF)
    k_ref[...] = keys
    v_ref[...] = values
    wq = wq_ref[...]
    q_ref[0 : 2 * PR, :] = (dot_nn(normed_ref[0 : 2 * PR, :], wq) * SCALE).astype(BF)
    q_ref[2 * PR :, :] = (dot_nn(normed_ref[PLEN:, :], wq) * SCALE).astype(BF)
    row = lax.broadcasted_iota(jnp.int32, (PR, PR), 0)
    col = lax.broadcasted_iota(jnp.int32, (PR, PR), 1)
    tri = jnp.where(col <= row, 0.0, neg_fill)
    for chunk in range(4):
        rows = slice(chunk * PR, (chunk + 1) * PR)
        query = q_ref[rows, :]
        outs, invs = [], []
        for head in range(2):
            masked = jnp.where(lane_half(head), query, jnp.zeros_like(query))
            scores = dot_nt(masked, k_ref[0:PLEN, :])
            if chunk < 2:
                scores = scores + bias_ref[rows, :]
                top = jnp.max(scores, axis=-1, keepdims=True)
                terms = jnp.exp(scores - top)
                total = jnp.sum(terms, axis=-1, keepdims=True)
                low_terms = terms.astype(BF)
                e_ref[head, rows, :] = low_terms
                out = dot_nn(low_terms, v_ref[0:PLEN, :])
            else:
                own = slice(PLEN + (chunk - 2) * PR, PLEN + (chunk - 1) * PR)
                near = dot_nt(masked, k_ref[own, :]) + tri
                top = jnp.maximum(
                    jnp.max(scores, axis=-1, keepdims=True), jnp.max(near, axis=-1, keepdims=True)
                )
                terms = jnp.exp(scores - top)
                near_terms = jnp.exp(near - top)
                total = jnp.sum(terms, axis=-1, keepdims=True) + jnp.sum(
                    near_terms, axis=-1, keepdims=True
                )
                low_terms = terms.astype(BF)
                low_near = near_terms.astype(BF)
                e_ref[head, rows, :] = low_terms
                ec_ref[head, (chunk - 2) * PR : (chunk - 1) * PR, :] = low_near
                out = dot_nn(low_terms, v_ref[0:PLEN, :]) + dot_nn(low_near, v_ref[own, :])
            inv = 1.0 / total
            outs.append(out * inv)
            invs.append(jnp.broadcast_to(inv, (PR, 2 * HDIM)))
        low_half = lane_half(0)
        o_ref[rows, :] = jnp.where(low_half, outs[0], outs[1]).astype(BF)
        r_ref[rows, :] = jnp.where(low_half, invs[0], invs[1])


def attn_fwd(pos, x_all, gain, w_qkv):
    pair = lambda n: (lambda i: (0, n * PAIRS + i))
    whole = lambda i: (0, 0)
    heads = lambda i: (i, 0, 0)
    width = 2 * HDIM
    return pl.pallas_call(
        attn_fwd_kernel,
        grid=(PAIRS,),
        in_specs=[
            pl.BlockSpec(memory_space=pltpu.SMEM),
            pl.BlockSpec((KEYS, D), whole),
            pl.BlockSpec((1, D), whole),
            pl.BlockSpec((D, width), pair(0)),
            pl.BlockSpec((D, width), pair(1)),
            pl.BlockSpec((D, width), pair(2)),
        ],
        out_specs=[
            pl.BlockSpec((ROWS, width), pair(0)),
            pl.BlockSpec((KEYS, width), pair(0)),
            pl.BlockSpec((KEYS, width), pair(0)),
            pl.BlockSpec((2, ROWS, PLEN), heads),
            pl.BlockSpec((2, 2 * PR, PR), heads),
            pl.BlockSpec((ROWS, width), pair(0)),
            pl.BlockSpec((ROWS, width), pair(0)),
        ],
        out_shape=[
            jax.ShapeDtypeStruct((ROWS, D), BF),
            jax.ShapeDtypeStruct((KEYS, D), BF),
            jax.ShapeDtypeStruct((KEYS, D), BF),
            jax.ShapeDtypeStruct((HEADS, ROWS, PLEN), BF),
            jax.ShapeDtypeStruct((HEADS, 2 * PR, PR), BF),
            jax.ShapeDtypeStruct((ROWS, D), BF),
            jax.ShapeDtypeStruct((ROWS, D), F32),
        ],
        scratch_shapes=[pltpu.VMEM((KEYS, D), BF), pltpu.VMEM((2 * PR, PLEN), F32)],
        compiler_params=pltpu.CompilerParams(vmem_limit_bytes=VMEM_LIMIT),
        cost_estimate=pl.CostEstimate(
            flops=20_000_000_000, bytes_accessed=25_000_000, transcendentals=6_300_000
        ),
    )(pos, x_all, gain, w_qkv, w_qkv, w_qkv)


def mlp_kernel(
    x_ref, att_ref, dout_ref, gain_ref, wout_ref, wup_ref, wdown_ref,
    out_ref, dmid_ref, datt_ref, dwout_ref, dwup_ref, dwdown_ref, dgain_ref,
    mid_ref, nm_ref, acc_ref, e_ref,
):
    step = pl.program_id(0)

    @pl.when(step == 0)
    def _():
        wout = wout_ref[...]
        gain = gain_ref[...]
        for chunk in range(4):
            rows = slice(chunk * PR, (chunk + 1) * PR)
            middle = x_ref[rows, :].astype(F32) + dot_nn(att_ref[rows, :], wout)
            mid_ref[rows, :] = middle
            nm_ref[rows, :] = (middle * rms_inv(middle) * gain).astype(BF)

    wup = wup_ref[...]
    wdown = wdown_ref[...]
    dout = dout_ref[...]
    hidden = dot_nn(nm_ref[...], wup)
    inner = GELU_C * (hidden + GELU_A * hidden * hidden * hidden)
    th = jnp.tanh(inner)
    active = (0.5 * hidden * (1.0 + th)).astype(BF)
    d_active = dot_nt(dout, wdown)
    slope = 0.5 * (1.0 + th) + 0.5 * hidden * (1.0 - th * th) * (
        GELU_C * (1.0 + 3.0 * GELU_A * hidden * hidden)
    )
    d_hidden = (d_active * slope).astype(BF)
    part_out = dot_nn(active, wdown)
    part_e = dot_nt(d_hidden, wup)

    @pl.when(step == 0)
    def _():
        acc_ref[...] = part_out
        e_ref[...] = part_e

    @pl.when(step > 0)
    def _():
        acc_ref[...] += part_out
        e_ref[...] += part_e

    dwdown_ref[...] = dot_tn(active, dout).astype(BF)
    dwup_ref[...] = dot_tn(nm_ref[...], d_hidden).astype(BF)

    @pl.when(step == pl.num_programs(0) - 1)
    def _():
        gain = gain_ref[...]
        wout = wout_ref[...]
        dgain = jnp.zeros((1, D), F32)
        for chunk in range(4):
            rows = slice(chunk * PR, (chunk + 1) * PR)
            middle = mid_ref[rows, :]
            out_ref[rows, :] = (middle + acc_ref[rows, :]).astype(BF)
            inv = rms_inv(middle)
            unit = middle * inv
            grad = e_ref[rows, :]
            scaled = gain * grad
            mean = jnp.mean(unit * scaled, axis=-1, keepdims=True)
            d_mid = dout_ref[rows, :].astype(F32) + inv * (scaled - unit * mean)
            dmid_ref[rows, :] = d_mid
            dgain = dgain + jnp.sum(grad * unit, axis=0, keepdims=True)
            branch = d_mid.astype(BF)
            nm_ref[rows, :] = branch
            datt_ref[rows, :] = dot_nt(branch, wout).astype(BF)
        dgain_ref[...] = dgain
        dwout_ref[...] = dot_tn(att_ref[...], nm_ref[...]).astype(BF)


def mlp(x_own, attended, d_out, gain, w_out, w_up, w_down):
    whole = lambda i: (0, 0)
    cols = lambda i: (0, i)
    down = lambda i: (i, 0)
    return pl.pallas_call(
        mlp_kernel,
        grid=(FF // FCHUNK,),
        in_specs=[
            pl.BlockSpec((ROWS, D), whole),
            pl.BlockSpec((ROWS, D), whole),
            pl.BlockSpec((ROWS, D), whole),
            pl.BlockSpec((1, D), whole),
            pl.BlockSpec((D, D), whole),
            pl.BlockSpec((D, FCHUNK), cols),
            pl.BlockSpec((FCHUNK, D), down),
        ],
        out_specs=[
            pl.BlockSpec((ROWS, D), whole),
            pl.BlockSpec((ROWS, D), whole),
            pl.BlockSpec((ROWS, D), whole),
            pl.BlockSpec((D, D), whole),
            pl.BlockSpec((D, FCHUNK), cols),
            pl.BlockSpec((FCHUNK, D), down),
            pl.BlockSpec((1, D), whole),
        ],
        out_shape=[
            jax.ShapeDtypeStruct((ROWS, D), BF),
            jax.ShapeDtypeStruct((ROWS, D), F32),
            jax.ShapeDtypeStruct((ROWS, D), BF),
            jax.ShapeDtypeStruct((D, D), BF),
            jax.ShapeDtypeStruct((D, FF), BF),
            jax.ShapeDtypeStruct((FF, D), BF),
            jax.ShapeDtypeStruct((1, D), F32),
        ],
        scratch_shapes=[
            pltpu.VMEM((ROWS, D), F32),
            pltpu.VMEM((ROWS, D), BF),
            pltpu.VMEM((ROWS, D), F32),
            pltpu.VMEM((ROWS, D), F32),
        ],
        compiler_params=pltpu.CompilerParams(vmem_limit_bytes=VMEM_LIMIT),
        cost_estimate=pl.CostEstimate(
            flops=17_000_000_000, bytes_accessed=27_000_000, transcendentals=1_600_000
        ),
    )(x_own, attended, d_out, gain, w_out, w_up, w_down)


def attn_bwd_kernel(
    x_ref, gain_ref, wq_ref, wk_ref, wv_ref, q_ref, k_ref, v_ref, e_ref, ec_ref, o_ref, r_ref,
    g_ref, dwq_ref, dwk_ref, dwv_ref, f_ref, dgain_ref,
    normed_ref, qs_ref, gs_ref, ds_ref, dk_ref, dv_ref, dq_ref,
):
    step = pl.program_id(0)

    @pl.when(step == 0)
    def _():
        fill_normed(x_ref, gain_ref, normed_ref)

    scaled_grad = g_ref[...].astype(F32) * r_ref[...]
    prod = scaled_grad * o_ref[...].astype(F32)
    low_grad = scaled_grad.astype(BF)
    query = q_ref[...]
    dq_parts = []
    for head in range(2):
        half = lane_half(head)
        grad_h = jnp.where(half, low_grad, jnp.zeros_like(low_grad))
        query_h = jnp.where(half, query, jnp.zeros_like(query))
        delta = jnp.sum(jnp.where(half, prod, 0.0), axis=-1, keepdims=True)
        gs_ref[...] = grad_h
        qs_ref[...] = query_h
        for chunk in range(4):
            rows = slice(chunk * PR, (chunk + 1) * PR)
            d_soft = dot_nt(gs_ref[rows, :], v_ref[0:PLEN, :])
            ds_ref[rows, :] = (
                e_ref[head, rows, :].astype(F32) * (d_soft - delta[rows])
            ).astype(BF)
        d_query = dot_nn(ds_ref[...], k_ref[0:PLEN, :])
        d_key = dot_tn(ds_ref[...], qs_ref[...])
        d_value = dot_tn(e_ref[head], gs_ref[...])
        near_q, near_k, near_v = [], [], []
        for part in range(2):
            own = slice(PLEN + part * PR, PLEN + (part + 1) * PR)
            mine = slice((2 + part) * PR, (3 + part) * PR)
            near = ec_ref[head, part * PR : (part + 1) * PR, :]
            d_soft = dot_nt(gs_ref[mine, :], v_ref[own, :])
            d_near = (near.astype(F32) * (d_soft - delta[mine])).astype(BF)
            near_q.append(dot_nn(d_near, k_ref[own, :]))
            near_k.append(dot_tn(d_near, qs_ref[mine, :]))
            near_v.append(dot_tn(near, gs_ref[mine, :]))
        dq_parts.append((d_query, near_q))
        if head == 0:
            dk_ref[0:PLEN, :] = d_key
            dv_ref[0:PLEN, :] = d_value
            for part in range(2):
                own = slice(PLEN + part * PR, PLEN + (part + 1) * PR)
                dk_ref[own, :] = near_k[part]
                dv_ref[own, :] = near_v[part]
        else:
            dk_ref[0:PLEN, :] += d_key
            dv_ref[0:PLEN, :] += d_value
            for part in range(2):
                own = slice(PLEN + part * PR, PLEN + (part + 1) * PR)
                dk_ref[own, :] += near_k[part]
                dv_ref[own, :] += near_v[part]
    low_half = lane_half(0)
    dq_ref[0 : 2 * PR, :] = (
        jnp.where(low_half, dq_parts[0][0][0 : 2 * PR], dq_parts[1][0][0 : 2 * PR]) * SCALE
    ).astype(BF)
    for part in range(2):
        mine = slice((2 + part) * PR, (3 + part) * PR)
        both = [dq_parts[h][0][mine] + dq_parts[h][1][part] for h in range(2)]
        dq_ref[mine, :] = (jnp.where(low_half, both[0], both[1]) * SCALE).astype(BF)
    d_key = dk_ref[...].astype(BF)
    d_value = dv_ref[...].astype(BF)
    d_query = dq_ref[...]
    dwk_ref[...] = dot_tn(normed_ref[...], d_key).astype(BF)
    dwv_ref[...] = dot_tn(normed_ref[...], d_value).astype(BF)
    dwq_ref[...] = (
        dot_tn(normed_ref[0 : 2 * PR, :], d_query[0 : 2 * PR])
        + dot_tn(normed_ref[PLEN:, :], d_query[2 * PR :])
    ).astype(BF)
    part_kv = dot_nt(d_key, wk_ref[...]) + dot_nt(d_value, wv_ref[...])
    part_q = dot_nt(d_query, wq_ref[...])

    @pl.when(step == 0)
    def _():
        f_ref[...] = part_kv

    @pl.when(step > 0)
    def _():
        f_ref[...] += part_kv

    f_ref[0 : 2 * PR, :] += part_q[0 : 2 * PR]
    f_ref[PLEN:, :] += part_q[2 * PR :]

    @pl.when(step == pl.num_programs(0) - 1)
    def _():
        total = jnp.zeros((1, D), F32)
        for block in range(KEYS // PR):
            rows = slice(block * PR, (block + 1) * PR)
            part = x_ref[rows, :].astype(F32)
            total = total + jnp.sum(f_ref[rows, :] * (part * rms_inv(part)), axis=0, keepdims=True)
        dgain_ref[...] = total


def attn_bwd(x_all, gain, w_qkv, saved, d_att):
    pair = lambda n: (lambda i: (0, n * PAIRS + i))
    whole = lambda i: (0, 0)
    heads = lambda i: (i, 0, 0)
    width = 2 * HDIM
    q, k, v, e, ec, o, r = saved
    return pl.pallas_call(
        attn_bwd_kernel,
        grid=(PAIRS,),
        in_specs=[
            pl.BlockSpec((KEYS, D), whole),
            pl.BlockSpec((1, D), whole),
            pl.BlockSpec((D, width), pair(0)),
            pl.BlockSpec((D, width), pair(1)),
            pl.BlockSpec((D, width), pair(2)),
            pl.BlockSpec((ROWS, width), pair(0)),
            pl.BlockSpec((KEYS, width), pair(0)),
            pl.BlockSpec((KEYS, width), pair(0)),
            pl.BlockSpec((2, ROWS, PLEN), heads),
            pl.BlockSpec((2, 2 * PR, PR), heads),
            pl.BlockSpec((ROWS, width), pair(0)),
            pl.BlockSpec((ROWS, width), pair(0)),
            pl.BlockSpec((ROWS, width), pair(0)),
        ],
        out_specs=[
            pl.BlockSpec((D, width), pair(0)),
            pl.BlockSpec((D, width), pair(0)),
            pl.BlockSpec((D, width), pair(0)),
            pl.BlockSpec((KEYS, D), whole),
            pl.BlockSpec((1, D), whole),
        ],
        out_shape=[
            jax.ShapeDtypeStruct((D, D), BF),
            jax.ShapeDtypeStruct((D, D), BF),
            jax.ShapeDtypeStruct((D, D), BF),
            jax.ShapeDtypeStruct((KEYS, D), F32),
            jax.ShapeDtypeStruct((1, D), F32),
        ],
        scratch_shapes=[
            pltpu.VMEM((KEYS, D), BF),
            pltpu.VMEM((ROWS, width), BF),
            pltpu.VMEM((ROWS, width), BF),
            pltpu.VMEM((ROWS, PLEN), BF),
            pltpu.VMEM((KEYS, width), F32),
            pltpu.VMEM((KEYS, width), F32),
            pltpu.VMEM((ROWS, width), BF),
        ],
        compiler_params=pltpu.CompilerParams(vmem_limit_bytes=VMEM_LIMIT),
        cost_estimate=pl.CostEstimate(
            flops=30_000_000_000, bytes_accessed=30_000_000, transcendentals=1000
        ),
    )(x_all, gain, w_qkv, w_qkv, w_qkv, q, k, v, e, ec, o, r, d_att)


def tail_kernel(x_ref, f_ref, dmid_ref, gain_ref, out_ref):
    gain = gain_ref[...]
    part = x_ref[...].astype(F32)
    inv = rms_inv(part)
    unit = part * inv
    scaled = gain * f_ref[...]
    mean = jnp.mean(unit * scaled, axis=-1, keepdims=True)
    out_ref[...] = dmid_ref[...] + inv * (scaled - unit * mean)


def tail(x_own, f_own, d_mid, gain):
    rows = lambda i: (i, 0)
    return pl.pallas_call(
        tail_kernel,
        grid=(4,),
        in_specs=[
            pl.BlockSpec((PR, D), rows),
            pl.BlockSpec((PR, D), rows),
            pl.BlockSpec((PR, D), rows),
            pl.BlockSpec((1, D), lambda i: (0, 0)),
        ],
        out_specs=pl.BlockSpec((PR, D), rows),
        out_shape=jax.ShapeDtypeStruct((ROWS, D), F32),
        compiler_params=pltpu.CompilerParams(vmem_limit_bytes=VMEM_LIMIT),
    )(x_own, f_own, d_mid, gain)


def xor_shard(value, bits):
    size = lax.axis_size("shard")
    return lax.ppermute(value, "shard", [(i, i ^ bits) for i in range(size)])


def part_of(values, start, rows=PR):
    return lax.dynamic_slice_in_dim(values, start, rows, 0)


def per_device(tokens, w_qkv, w_out, w_up, w_down, gain_attn, gain_mlp, d_out):
    shards = lax.axis_size("shard")
    shard = lax.axis_index("shard")
    pos = shard % 8
    side = pos % 2

    def swap(values):
        mine_p = part_of(values, side * PR)
        mine_c = part_of(values, (2 + side) * PR)
        give = jnp.concatenate(
            [part_of(values, (1 - side) * PR), part_of(values, (3 - side) * PR)], axis=0
        )
        got = xor_shard(give, 1)
        return jnp.concatenate([mine_p, got[:PR], mine_c, got[PR:]], axis=0)

    def swap_back(values):
        got = xor_shard(
            jnp.concatenate([values[PR : 2 * PR], values[3 * PR :]], axis=0).astype(BF), 1
        ).astype(values.dtype)
        mine_p, mine_c = values[:PR], values[2 * PR : 3 * PR]
        first = side == 0
        return jnp.concatenate(
            [
                jnp.where(first, mine_p, got[:PR]),
                jnp.where(first, got[:PR], mine_p),
                jnp.where(first, mine_c, got[PR:]),
                jnp.where(first, got[PR:], mine_c),
            ],
            axis=0,
        )

    full_qkv = lax.all_gather(w_qkv, "shard", axis=0, tiled=True)
    full_gain_attn = lax.all_gather(gain_attn, "shard", axis=0, tiled=True)
    full_gain_mlp = lax.all_gather(gain_mlp, "shard", axis=0, tiled=True)
    full_out = lax.all_gather(w_out, "shard", axis=0, tiled=True)
    full_up = lax.all_gather(w_up, "shard", axis=0, tiled=True)
    full_down = lax.all_gather(w_down, "shard", axis=0, tiled=True)
    attn_gain = full_gain_attn.astype(F32).reshape(1, D)
    mlp_gain = full_gain_mlp.astype(F32).reshape(1, D)

    x_own = swap(tokens)
    g_own = swap(d_out)
    near = x_own[: 2 * PR]
    others = [xor_shard(near, 2 * k) for k in range(1, 4)]
    x_all = jnp.concatenate([near] + others + [x_own[2 * PR :]], axis=0)

    saved = attn_fwd(pos.reshape(1).astype(jnp.int32), x_all, attn_gain, full_qkv)
    attended = saved[5]
    block_rows, d_mid, d_att, d_wout, d_wup, d_wdown, d_gain_mlp = mlp(
        x_own, attended, g_own, mlp_gain, full_out, full_up, full_down
    )
    block_out = swap_back(block_rows)
    d_wq, d_wk, d_wv, f_all, d_gain_attn = attn_bwd(x_all, attn_gain, full_qkv, saved, d_att)
    f_near = f_all[: 2 * PR]
    for k in range(1, 4):
        sent = f_all[2 * k * PR : 2 * (k + 1) * PR].astype(BF)
        f_near = f_near + xor_shard(sent, 2 * k).astype(F32)
    f_own = jnp.concatenate([f_near, f_all[PLEN:]], axis=0)
    d_tokens = swap_back(tail(x_own, f_own, d_mid, attn_gain))

    d_wqkv = jnp.concatenate([d_wq, d_wk, d_wv], axis=1)

    def reduce(grad):
        part = lax.psum_scatter(grad, "shard", scatter_dimension=0, tiled=True)
        return lax.psum(part, "rep").astype(F32)

    return (
        block_out,
        d_tokens,
        reduce(d_wqkv),
        reduce(d_wout),
        reduce(d_wup),
        reduce(d_wdown),
        lax.psum(lax.psum_scatter(d_gain_attn.reshape(D), "shard", scatter_dimension=0, tiled=True), "rep"),
        lax.psum(lax.psum_scatter(d_gain_mlp.reshape(D), "shard", scatter_dimension=0, tiled=True), "rep"),
    )


def solution(mesh):
    weights = P("shard", None)
    rows = P(("rep", "shard"), None)
    return jax.shard_map(
        per_device,
        mesh=mesh,
        in_specs=(rows, weights, weights, weights, weights, P("shard"), P("shard"), rows),
        out_specs=(rows, rows, weights, weights, weights, weights, P("shard"), P("shard")),
        check_vma=False,
    )
```

time: 1180 us -> 768 us (0.65)
  waiting for transfers between devices: 805 us -> 542 us
  matrix products: 160 us -> 0 us
  Pallas kernels: 0 us -> 112 us
  other arithmetic: 93 us -> 20.4 us
  local copies, waits for them, and re-layouts: 50.3 us -> 8.58 us
    ppermute x6 -> x10, waiting for transfers between devices: 536 us -> 121 us  [xor_shard(): return lax.ppermute(value, 'shard', [(i, i ^ bits) for i in range(size)])]
    dot_general x18 -> x0, matrix products: 160 us -> none  [the longest x1 26.4 us: attend_back(): jnp.einsum('brhd,bkhd->bhrk', grad_heads, value_heads, preferred_element_...]
    pallas_call x0 -> x4, Pallas kernels: none -> 112 us  [the longest x1 46.7 us: attn_bwd(): pl.pallas_call(attn_bwd_kernel, grid=(PAIRS,), in_specs=[pl.BlockSpec((KE...]
    all_gather x4, waiting for transfers between devices: 82.1 us -> 164 us  [the longest x1 80.9 us: per_device(): full_up = lax.all_gather(w_up, 'shard', axis=0, tiled=True)]
    reduce_scatter x4, waiting for transfers between devices: 175 us -> 238 us  [reduce(): part = lax.psum_scatter(grad, 'shard', scatter_dimension=0, tiled=True)]
    convert_element_type x16 -> x5, other arithmetic: 44.7 us -> 6.01 us  [the longest x4 5.95 us: reduce(): return lax.psum(part, 'rep').astype(F32)]
    slice x11 -> x5, local copies, waits for them, and re-layouts: 19.3 us -> 0.85 us  [the longest x2 0.71 us: swap(): return jnp.concatenate([mine_p, got[:PR], mine_c, got[PR:]], axis=0)]
    reshape x2, local copies, waits for them, and re-layouts: 16.4 us -> 1.18 us  [the longest x1 0.6 us: per_device(): mlp_gain = full_gain_mlp.astype(F32).reshape(1, D)]
  transfers between devices with their start and end apart: 15 -> 19, of which waited for: 11 -> 12; matrix products, arithmetic and copies ran while one was open for 23% -> 3% of each run, Pallas kernels for 0% -> 11%
where the time goes in v1:
time: 768 us
  waiting for transfers between devices  542 us (71%)
  Pallas kernels  112 us (15%)
  blocking collectives  57.8 us (8%)
  other arithmetic  20.4 us (3%)
  between operations  15.4 us (2%)
  starting transfers between devices  11.1 us (1%)
  local copies, waits for them, and re-layouts  8.58 us (1%)
    reduce_scatter x4, waiting for transfers between devices, reduce(): part = lax.psum_scatter(grad, 'shard', scatter_dimension=0, tiled=True)  238 us
    ppermute x10, waiting for transfers between devices, xor_shard(): return lax.ppermute(value, 'shard', [(i, i ^ bits) for i in range(size)])  121 us
    all_gather x1, waiting for transfers between devices, per_device(): full_up = lax.all_gather(w_up, 'shard', axis=0, tiled=True)  80.9 us
    all_gather x1, waiting for transfers between devices, per_device(): full_down = lax.all_gather(w_down, 'shard', axis=0, tiled=True)  80.1 us
    unnamed x2, blocking collectives  51.6 us
    pallas_call x1, Pallas kernels, attn_bwd(): pl.pallas_call(attn_bwd_kernel, grid=(PAIRS,), in_specs=[pl.BlockSpec((KE...  46.7 us
    pallas_call x1, Pallas kernels, attn_fwd(): pl.pallas_call(attn_fwd_kernel, grid=(PAIRS,), in_specs=[pl.BlockSpec(mem...  31.8 us
    pallas_call x1, Pallas kernels, mlp(): pl.pallas_call(mlp_kernel, grid=(FF // FCHUNK,), in_specs=[pl.BlockSpec((...  29.4 us
  transfers between devices with their start and end apart: 19, of which 12 were waited for; matrix products, arithmetic and copies ran while one was open for 3% of the time, Pallas kernels for 11%

profile of v1, /device:TPU:0, one launch (start us, length us, event | category | flops | bytes accessed | tf_op | source)
XLA Modules:
  0.0 767.9 jit_solution(2367876028266067480)
XLA Ops:
  10.9 3.0 collective-permute-start
  14.1 11.2 %collective-permute-done = bf16[256,768]{1,0:T(8,128)(2,1)S(1)} collective-permute-done((bf16[256,768]{1,0:T(8,128)(2,1)S(1)}, bf16[256,768]{1,0:T(8,128)(2,1)S(1)}, u32[]{:S(2)}, u32[]{:S(2)}) %collective-permute-start) | collective-permute-done | bytes 393248 | tf_op jit(solution)/shard_map/ppermute | solution.py:471
  29.2 29.6 %all-reduce.6 = (bf16[768]{0:T(1024)(128)(2,1)S(1)}, bf16[768]{0:T(1024)(128)(2,1)S(1)}) all-reduce(bf16[768]{0:T(1024)(128)(2,1)S(1)} %dynamic-update-slice, bf16[768]{0:T(1024)(128)(2,1)S(1)} %dynamic-update-slice.1), channel_id=1, replica_groups=mesh['rep'=4,'shard'=8] {'shard'}, use_global_device_ids=true, to_apply=%add | all-reduce | flops 1536 | bytes 6144
  62.0 55.5 %collective-permute-done.2 = bf16[256,768]{1,0:T(8,128)(2,1)S(1)} collective-permute-done((bf16[256,768]{1,0:T(8,128)(2,1)S(1)}, bf16[256,768]{1,0:T(8,128)(2,1)S(1)}, u32[]{:S(2)}, u32[]{:S(2)}) %collective-permute-start.2) | collective-permute-done | bytes 393248 | tf_op jit(solution)/shard_map/ppermute | solution.py:471
  121.5 31.8 %shard_map.143 = (bf16[512,768]{1,0:T(8,128)(2,1)}, bf16[1280,768]{1,0:T(8,128)(2,1)}, bf16[1280,768]{1,0:T(8,128)(2,1)}, bf16[12,512,1024]{2,1,0:T(8,128)(2,1)}...) custom-call(s32[1]{0:T(128)} %bitcast.pos_ref, ...), custom_call_target="tpu_custom_call" | custom-call | flops 20000000000 | bytes 25000000 | tf_op jit(solution)/shard_map/pallas_call | solution.py:137
  153.3 3.4 all-gather.7.cloned.1.call-done.wout_ref
  156.6 80.9 %all-gather.9.cloned.1.call-done.wup_ref = bf16[768,3072]{1,0:T(8,128)(2,1)} async-done(((bf16[96,3072]{1,0:T(8,128)(2,1)}), bf16[768,3072]{1,0:T(8,128)(2,1)}) %all-gather.9.cloned.1.call-update) | async-done | bytes 4718608 | tf_op jit(solution)/shard_map/all_gather | solution.py:513
  237.5 80.1 %all-gather.11.cloned.1.call-done.wdown_ref = bf16[3072,768]{1,0:T(8,128)(2,1)} async-done(((bf16[384,768]{1,0:T(8,128)(2,1)}), bf16[3072,768]{1,0:T(8,128)(2,1)}) %all-gather.11.cloned.1.call-update) | async-done | bytes 4718608 | tf_op jit(solution)/shard_map/all_gather | solution.py:514
  317.6 29.4 %shard_map.144 = (bf16[512,768]{1,0:T(8,128)(2,1)}, f32[512,768]{1,0:T(8,128)}, bf16[512,768]{1,0:T(8,128)(2,1)}, bf16[768,768]{1,0:T(8,128)(2,1)}, bf16[768,307...) custom-call(bf16[512,768]{1,0:T(8,128)(2,1)} %pad_maximum_fusion.3.x_ref, ...), custom_call_target="tpu_custom_call" | custom-call | flops 16999999488 | bytes 27000000 | tf_op jit(solution)/shard_map/pallas_call | solution.py:247
  347.3 46.7 %shard_map.145 = (bf16[768,768]{1,0:T(8,128)(2,1)}, bf16[768,768]{1,0:T(8,128)(2,1)}, bf16[768,768]{1,0:T(8,128)(2,1)}, f32[1280,768]{1,0:T(8,128)}, f32[1,768]{1,0:T(1,128)}) custom-call(bf16[1280,768]{1,0:T(8,128)(2,1)} %get-tuple-element.85.x_ref, f32[1,768]{1,0:T(1,128)} %reshape.43.gain_ref, ...), custom_call_target="tpu_custom_call" | custom-call | flops 30000001024 | bytes 30000000 | tf_op jit(solution)/shard_map/pallas_call | solution.py:394
  394.0 3.3 pad_maximum_fusion
  398.9 2.3 convert.13
  401.9 2.4 collective-permute-start.8
  405.5 8.9 %collective-permute-done.6 = bf16[256,768]{1,0:T(8,128)(2,1)S(1)} collective-permute-done((bf16[256,768]{1,0:T(8,128)(2,1)S(1)}, bf16[256,768]{1,0:T(8,128)(2,1)S(1)}, u32[]{:S(2)}, u32[]{:S(2)}) %collective-permute-start.6) | collective-permute-done | bytes 393248 | tf_op jit(solution)/shard_map/ppermute | solution.py:471
  414.4 10.1 %collective-permute-done.8 = bf16[256,768]{1,0:T(8,128)(2,1)S(1)} collective-permute-done((bf16[256,768]{1,0:T(8,128)(2,1)S(1)}, bf16[256,768]{1,0:T(8,128)(2,1)S(1)}, u32[]{:S(2)}, u32[]{:S(2)}) %collective-permute-start.8) | collective-permute-done | bytes 393248 | tf_op jit(solution)/shard_map/ppermute | solution.py:471
  424.5 34.9 %collective-permute-done.7 = bf16[256,768]{1,0:T(8,128)(2,1)S(1)} collective-permute-done((bf16[256,768]{1,0:T(8,128)(2,1)S(1)}, bf16[256,768]{1,0:T(8,128)(2,1)S(1)}, u32[]{:S(2)}, u32[]{:S(2)}) %collective-permute-start.7) | collective-permute-done | bytes 393248 | tf_op jit(solution)/shard_map/ppermute | solution.py:471
  462.3 4.5 shard_map.146
  468.4 40.9 %reduce-scatter.5.cloned.1.call-done = bf16[96,2304]{1,0:T(8,128)(2,1)} async-done(((bf16[768,2304]{1,0:T(8,128)(2,1)}), bf16[96,2304]{1,0:T(8,128)(2,1)}) %reduce-scatter.5.cloned.1.call-update) | async-done | bytes 442384 | tf_op jit(solution)/shard_map/reduce_scatter | solution.py:541
  509.3 98.5 %reduce-scatter.9.cloned.1.call-done = bf16[96,3072]{1,0:T(8,128)(2,1)} async-done(((bf16[768,3072]{1,0:T(8,128)(2,1)}), bf16[96,3072]{1,0:T(8,128)(2,1)}) %reduce-scatter.9.cloned.1.call-update) | async-done | bytes 589840 | tf_op jit(solution)/shard_map/reduce_scatter | solution.py:541
  607.7 98.7 %reduce-scatter.11.cloned.1.call-done = bf16[384,768]{1,0:T(8,128)(2,1)} async-done(((bf16[3072,768]{1,0:T(8,128)(2,1)}), bf16[384,768]{1,0:T(8,128)(2,1)}) %reduce-scatter.11.cloned.1.call-update) | async-done | bytes 589840 | tf_op jit(solution)/shard_map/reduce_scatter | solution.py:541
  708.8 22.0 %all-reduce.4 = (f32[768]{0:T(1024)S(1)}, f32[768]{0:T(1024)S(1)}) all-reduce(f32[768]{0:T(1024)S(1)} %reduce, f32[768]{0:T(1024)S(1)} %reduce.1), channel_id=6, replica_groups=mesh['rep'=4,'shard'=8] {'shard'}, use_global_device_ids=true, to_apply=%region_8.9.clone | all-reduce | flops 1536 | bytes 12288
  730.9 6.1 all-reduce.5
  740.3 15.2 %all-reduce.10.cloned.1.call-done = (bf16[96,2304]{1,0:T(8,128)(2,1)}, bf16[96,768]{1,0:T(8,128)(2,1)}, bf16[96,3072]{1,0:T(8,128)(2,1)}, bf16[384,768]{1,0:T(8,128)(2,1)}) async-done(((bf16[96,2304]{1,0:T(8,128)(2,1)}, bf16[96,768]{1,0:T(8,128)(2,1)}, bf16[96,3072]{1,0:T(8,128)(2,1)}, bf16[384,768]{1,0:T(8,128)(2,1)}), (bf16[96,2304]{1,0:T(8,128)(2,1)}, bf16[96,768]{1,0:T(8,128)(2,1)}, ...) | async-done | bytes 1769488 | tf_op jit(solution)/shard_map/psum | solution.py:542
  757.1 2.0 convert_element_type.34
  (95 shorter events, 31.0 us)
Async XLA Ops:
  7.2 114.3 %all-gather.5.cloned.1.call-start = ((), (), s32[]{:S(2)}) async-start(), calls=%async_computation.4 | async-start | bytes 3981312 | tf_op jit(solution)/shard_map/all_gather | solution.py:509
  7.9 148.7 %all-gather.7.cloned.1.call-start = ((), (), s32[]{:S(2)}) async-start(), calls=%async_computation.5 | async-start | bytes 1327104 | tf_op jit(solution)/shard_map/all_gather | solution.py:512
  8.7 228.9 %all-gather.9.cloned.1.call-start = ((), (), s32[]{:S(2)}) async-start(), calls=%async_computation.6 | async-start | bytes 5308416 | tf_op jit(solution)/shard_map/all_gather | solution.py:513
  9.4 308.2 %all-gather.11.cloned.1.call-start = ((), (), s32[]{:S(2)}) async-start(), calls=%async_computation.7 | async-start | bytes 5308416 | tf_op jit(solution)/shard_map/all_gather | solution.py:514
  10.0 458.4 %reduce-scatter.7.cloned.1.call-start = ((), (), s32[]{:S(2)}) async-start(), calls=%async_computation.9 | async-start | bytes 1327104 | tf_op jit(solution)/shard_map/reduce_scatter | solution.py:541
  10.9 16.6 %copy-start.8 = (u32[32]{0:T(128)S(1)}, u32[32]{0:T(128)}, u32[]{:S(2)}) copy-start(u32[32]{0:T(128)} %constant.37) | copy-start | bytes 388
  10.9 17.9 %copy-start.9 = (bf16[96]{0:T(256)(128)(2,1)S(1)}, bf16[96]{0:T(256)(128)(2,1)}, u32[]{:S(2)}) copy-start(bf16[96]{0:T(256)(128)(2,1)} %param.13) | copy-start | bytes 580
  10.9 18.1 %copy-start.10 = (bf16[96]{0:T(256)(128)(2,1)S(1)}, bf16[96]{0:T(256)(128)(2,1)}, u32[]{:S(2)}) copy-start(bf16[96]{0:T(256)(128)(2,1)} %param.14) | copy-start | bytes 580
  10.9 14.4 %collective-permute-start = (bf16[256,768]{1,0:T(8,128)(2,1)S(1)}, bf16[256,768]{1,0:T(8,128)(2,1)S(1)}, u32[]{:S(2)}, u32[]{:S(2)}) collective-permute-start(bf16[256,768]{1,0:T(8,128)(2,1)S(1)} %pad_maximum_fusion.6), channel_id=1, source_target_pairs={{0,1},{1,0},{2,3},{3,2},{4,5},{5,4},{6,7},{7,6},{8,9},{9,8},{10,11... | collective-permute-start | bytes 1179656 | tf_op jit(solution)/shard_map/ppermute | solution.py:471
  14.0 46.3 %collective-permute-start.4 = (bf16[256,768]{1,0:T(8,128)(2,1)S(1)}, bf16[256,768]{1,0:T(8,128)(2,1)S(1)}, u32[]{:S(2)}, u32[]{:S(2)}) collective-permute-start(bf16[256,768]{1,0:T(8,128)(2,1)S(1)} %pad_maximum_fusion.8), channel_id=1, source_target_pairs={{0,1},{1,0},{2,3},{3,2},{4,5},{5,4},{6,7},{7,6},{8,9},{9,8},{10,11... | collective-permute-start | bytes 1179656 | tf_op jit(solution)/shard_map/ppermute | solution.py:471
  26.0 35.2 %collective-permute-start.1 = (bf16[256,768]{1,0:T(8,128)(2,1)S(1)}, bf16[256,768]{1,0:T(8,128)(2,1)S(1)}, u32[]{:S(2)}, u32[]{:S(2)}) collective-permute-start(bf16[256,768]{1,0:T(8,128)(2,1)S(1)} %pad_maximum_fusion.7), channel_id=1, source_target_pairs={{0,2},{1,3},{2,0},{3,1},{4,6},{5,7},{6,4},{7,5},{8,10},{9,11},{10,... | collective-permute-start | bytes 1179656 | tf_op jit(solution)/shard_map/ppermute | solution.py:471
  60.1 58.3 %collective-permute-start.3 = (bf16[256,768]{1,0:T(8,128)(2,1)S(1)}, bf16[256,768]{1,0:T(8,128)(2,1)S(1)}, u32[]{:S(2)}, u32[]{:S(2)}) collective-permute-start(bf16[256,768]{1,0:T(8,128)(2,1)S(1)} %pad_maximum_fusion.7), channel_id=1, source_target_pairs={{0,6},{1,7},{2,4},{3,5},{4,2},{5,3},{6,0},{7,1},{8,14},{9,15},{10,... | collective-permute-start | bytes 1179656 | tf_op jit(solution)/shard_map/ppermute | solution.py:471
  60.1 57.5 %collective-permute-start.2 = (bf16[256,768]{1,0:T(8,128)(2,1)S(1)}, bf16[256,768]{1,0:T(8,128)(2,1)S(1)}, u32[]{:S(2)}, u32[]{:S(2)}) collective-permute-start(bf16[256,768]{1,0:T(8,128)(2,1)S(1)} %pad_maximum_fusion.7), channel_id=1, source_target_pairs={{0,4},{1,5},{2,6},{3,7},{4,0},{5,1},{6,2},{7,3},{8,12},{9,13},{10,... | collective-permute-start | bytes 1179656 | tf_op jit(solution)/shard_map/ppermute | solution.py:471
  347.1 162.2 %reduce-scatter.5.cloned.1.call-start = ((), (), s32[]{:S(2)}) async-start(), calls=%async_computation.8 | async-start | bytes 3981312 | tf_op jit(solution)/shard_map/reduce_scatter | solution.py:541
  397.4 210.4 %reduce-scatter.9.cloned.1.call-start = ((), (), s32[]{:S(2)}) async-start(), calls=%async_computation.10 | async-start | bytes 5308416 | tf_op jit(solution)/shard_map/reduce_scatter | solution.py:541
  398.1 308.3 %reduce-scatter.11.cloned.1.call-start = ((), (), s32[]{:S(2)}) async-start(), calls=%async_computation.11 | async-start | bytes 5308416 | tf_op jit(solution)/shard_map/reduce_scatter | solution.py:541
  398.9 356.6 %all-reduce.10.cloned.1.call-start = ((), (), s32[]{:S(2)}) async-start(), calls=%async_computation.12 | async-start | bytes 3538944 | tf_op jit(solution)/shard_map/psum | solution.py:542
  401.3 13.1 %collective-permute-start.6 = (bf16[256,768]{1,0:T(8,128)(2,1)S(1)}, bf16[256,768]{1,0:T(8,128)(2,1)S(1)}, u32[]{:S(2)}, u32[]{:S(2)}) collective-permute-start(bf16[256,768]{1,0:T(8,128)(2,1)S(1)} %get-tuple-element.66), channel_id=1, source_target_pairs={{0,2},{1,3},{2,0},{3,1},{4,6},{5,7},{6,4},{7,5},{8,10},{9,11},{10,... | collective-permute-start | bytes 1179656 | tf_op jit(solution)/shard_map/ppermute | solution.py:471
  401.9 22.7 %collective-permute-start.8 = (bf16[256,768]{1,0:T(8,128)(2,1)S(1)}, bf16[256,768]{1,0:T(8,128)(2,1)S(1)}, u32[]{:S(2)}, u32[]{:S(2)}) collective-permute-start(bf16[256,768]{1,0:T(8,128)(2,1)S(1)} %get-tuple-element.67), channel_id=1, source_target_pairs={{0,6},{1,7},{2,4},{3,5},{4,2},{5,3},{6,0},{7,1},{8,14},{9,15},{10,... | collective-permute-start | bytes 1179656 | tf_op jit(solution)/shard_map/ppermute | solution.py:471
  404.3 55.2 %collective-permute-start.7 = (bf16[256,768]{1,0:T(8,128)(2,1)S(1)}, bf16[256,768]{1,0:T(8,128)(2,1)S(1)}, u32[]{:S(2)}, u32[]{:S(2)}) collective-permute-start(bf16[256,768]{1,0:T(8,128)(2,1)S(1)} %get-tuple-element.68), channel_id=1, source_target_pairs={{0,4},{1,5},{2,6},{3,7},{4,0},{5,1},{6,2},{7,3},{8,12},{9,13},{10,... | collective-permute-start | bytes 1179656 | tf_op jit(solution)/shard_map/ppermute | solution.py:471
  404.9 332.1 %collective-permute-start.5 = (bf16[256,768]{1,0:T(8,128)(2,1)S(1)}, bf16[256,768]{1,0:T(8,128)(2,1)S(1)}, u32[]{:S(2)}, u32[]{:S(2)}) collective-permute-start(bf16[256,768]{1,0:T(8,128)(2,1)S(1)} %pad_maximum_fusion.9), channel_id=1, source_target_pairs={{0,1},{1,0},{2,3},{3,2},{4,5},{5,4},{6,7},{7,6},{8,9},{9,8},{10,11... | collective-permute-start | bytes 1179656 | tf_op jit(solution)/shard_map/ppermute | solution.py:471
  468.3 240.4 %copy-start.7 = (f32[1,768]{1,0:T(1,128)S(1)}, f32[1,768]{1,0:T(1,128)}, u32[]{:S(2)}) copy-start(f32[1,768]{1,0:T(1,128)} %get-tuple-element.44) | copy-start | bytes 9220
  468.3 240.4 %copy-start.6 = (f32[1,768]{1,0:T(1,128)S(1)}, f32[1,768]{1,0:T(1,128)}, u32[]{:S(2)}) copy-start(f32[1,768]{1,0:T(1,128)} %get-tuple-element.45) | copy-start | bytes 9220
  706.5 31.6 %collective-permute-start.9 = (bf16[256,768]{1,0:T(8,128)(2,1)S(1)}, bf16[256,768]{1,0:T(8,128)(2,1)S(1)}, u32[]{:S(2)}, u32[]{:S(2)}) collective-permute-start(bf16[256,768]{1,0:T(8,128)(2,1)S(1)} %pad_maximum_fusion.10), channel_id=1, source_target_pairs={{0,1},{1,0},{2,3},{3,2},{4,5},{5,4},{6,7},{7,6},{8,9},{9,8},{10,11... | collective-permute-start | bytes 1179656 | tf_op jit(solution)/shard_map/ppermute | solution.py:471
  (6 other events, 18.2 us)
Sparse Core Ops, SparseCore 0:
  10.2 103.7 all-gather.4
  116.2 40.4 all-gather.6
  158.8 78.6 all-gather.8
  239.6 78.0 all-gather.10
  347.2 63.5 reduce-scatter.6
  414.3 94.9 reduce-scatter.4
  512.9 94.7 reduce-scatter.8
  611.4 95.0 reduce-scatter.10
  709.0 46.3 all-reduce.9
